TPU v7x, 32 devices: a whole 2x2x4 slice. The times are simulated.
32 devices in a mesh: rep: 4 (over x, core), fsdp: 8 (over z, y).
Axes of the slice: x: 2, y: 2, z: 4, core: 2. Of those that a mesh axis runs over, the one named last changes fastest.
Arguments:
- replica_grads: bfloat16 [4, 8192, 8192], P('rep', 'fsdp'), may hold values from -0.19921875 to 0.19921875
- weight: bfloat16 [8192, 8192], P('fsdp'), may hold values from -6 to 6
- moment_one: float32 [1024, 1024], P('rep', 'fsdp'), may hold values from -3 to 3
- moment_two: float32 [1024, 1024], P('rep', 'fsdp'), may hold values from 0.1 to 10
- sign_bits: int32 [8192], replicated, may hold values from 0 to 1
- kept_rows: int32 [1024], replicated, may hold values from 0 to 8191, as said below
- step_count: int32 [], replicated, may hold values from 1 to 7
Outputs:
- new_weight: bfloat16 [8192, 8192], P('fsdp')
- new_moment_one: float32 [1024, 1024], P('rep', 'fsdp')
- new_moment_two: float32 [1024, 1024], P('rep', 'fsdp')
Inputs may be any that keep to these rules, and one draw needn't show every extreme that they name: `kept_rows`: all different; 0 and 8191 are always among them.
All inputs are finite; a program needn't handle non-finite values.
Results may differ from a plain program's by a relative error of at most 0.0049.
Values may be sent and summed in bfloat16 or wider, within the bound.
A program may use at most 192 MiB of HBM per device.

v0:
```python
import math

import jax
import jax.numpy as jnp
from jax import lax
from jax.sharding import PartitionSpec as P

BETA_ONE = 0.9
BETA_TWO = 0.95
EPSILON = 1e-08
LEARN_RATE = 0.25


def hadamard(order):
    positions = jnp.arange(order, dtype=jnp.int32)
    both = jnp.bitwise_and(positions[:, None], positions[None, :])
    parity = jnp.zeros_like(both)
    for bit_index in range(max(order.bit_length() - 1, 0)):
        parity = parity + jnp.bitwise_and(jnp.right_shift(both, bit_index), 1)
    parity = parity % 2
    return (1 - 2 * parity).astype(jnp.float32)


def transform_last(matrix):
    length = matrix.shape[-1]
    low_len = min(length, 128)
    high_len = length // low_len
    values = matrix.reshape(matrix.shape[:-1] + (high_len, low_len))
    if matrix.dtype == jnp.bfloat16:
        values = jnp.einsum(
            "rab,cb->rac",
            values,
            hadamard(low_len).astype(jnp.bfloat16),
            preferred_element_type=jnp.float32,
        )
    else:
        values = jnp.einsum(
            "rab,cb->rac", values, hadamard(low_len), precision=lax.Precision.HIGHEST
        )
    values = jnp.einsum("rab,ca->rcb", values, hadamard(high_len), precision=lax.Precision.HIGHEST)
    return values.reshape(matrix.shape)


def transform_rows(matrix):
    length = matrix.shape[0]
    low_len = min(length, 128)
    high_len = length // low_len
    values = matrix.reshape((high_len, low_len) + matrix.shape[1:])
    values = jnp.einsum("abc,db->adc", values, hadamard(low_len), precision=lax.Precision.HIGHEST)
    values = jnp.einsum("abc,da->dbc", values, hadamard(high_len), precision=lax.Precision.HIGHEST)
    return values.reshape(matrix.shape)


def local(replica_grads, weight, moment_one, moment_two, sign_bits, kept_rows, step_count):
    sign_vec = (1 - 2 * sign_bits).astype(jnp.float32)
    full_len = sign_vec.shape[0]
    kept_len = kept_rows.shape[0]
    norm_scale = 1.0 / math.sqrt(kept_len)
    row_count = moment_one.shape[0]
    local_grads = replica_grads[0]
    summed = lax.psum_scatter(
        local_grads.astype(jnp.float32).astype(jnp.bfloat16), "rep", scatter_dimension=0, tiled=True
    ).astype(jnp.float32)
    row_part = jnp.take(transform_last(summed * sign_vec[None, :]), kept_rows, axis=1) * norm_scale
    row_block = lax.all_gather(row_part.astype(jnp.bfloat16), "rep", axis=0, tiled=True).astype(
        row_part.dtype
    )
    col_panel = lax.all_to_all(
        row_block.astype(jnp.bfloat16), "fsdp", split_axis=1, concat_axis=0, tiled=True
    ).astype(row_block.dtype)
    col_sketch = (
        jnp.take(transform_rows(col_panel * sign_vec[:, None]), kept_rows, axis=0) * norm_scale
    )
    start_row = lax.axis_index("rep") * row_count
    compressed = lax.dynamic_slice_in_dim(col_sketch, start_row, row_count, 0)
    new_one = BETA_ONE * moment_one + (1.0 - BETA_ONE) * compressed
    new_two = BETA_TWO * moment_two + (1.0 - BETA_TWO) * compressed * compressed
    steps_done = step_count.astype(jnp.float32)
    first_fix = 1.0 - jnp.power(jnp.float32(BETA_ONE), steps_done)
    second_fix = 1.0 - jnp.power(jnp.float32(BETA_TWO), steps_done)
    direction = new_one / first_fix / (jnp.sqrt(new_two / second_fix) + EPSILON)
    dir_panel = lax.all_gather(direction, "rep", axis=0, tiled=True)
    placed = jnp.zeros((full_len, dir_panel.shape[1]), jnp.float32).at[kept_rows].set(dir_panel)
    back_bf = (transform_rows(placed) * sign_vec[:, None] * norm_scale).astype(jnp.bfloat16)
    back_rows = lax.all_to_all(back_bf, "fsdp", split_axis=0, concat_axis=1, tiled=True)
    col_fill = (
        jnp.zeros((back_rows.shape[0], full_len), jnp.bfloat16).at[:, kept_rows].set(back_rows)
    )
    update_full = transform_last(col_fill) * sign_vec[None, :] * norm_scale
    new_weight = (weight.astype(jnp.float32) - LEARN_RATE * update_full).astype(jnp.bfloat16)
    return (new_weight, new_one, new_two)


def solution(mesh):
    in_specs = (
        P("rep", "fsdp", None),
        P("fsdp", None),
        P("rep", "fsdp"),
        P("rep", "fsdp"),
        P(),
        P(),
        P(),
    )
    out_specs = (P("fsdp", None), P("rep", "fsdp"), P("rep", "fsdp"))
    return jax.shard_map(local, mesh=mesh, in_specs=in_specs, out_specs=out_specs, check_vma=False)
```

profile of v0, /device:TPU:31, one launch (start us, length us, event | category | flops | bytes accessed | tf_op | source)
XLA Modules:
  0.0 487.9 jit_solution(15517803826106365122)
XLA Ops:
  7.2 0.7 reduce-scatter.2.cloned.1.call-update
  8.0 128.8 %reduce-scatter.2.cloned.1.call-done = bf16[256,8192]{1,0:T(8,128)(2,1)} async-done(((bf16[1024,8192]{1,0:T(8,128)(2,1)}), bf16[256,8192]{1,0:T(8,128)(2,1)}) %reduce-scatter.2.cloned.1.call-update) | async-done | bytes 4194320 | tf_op jit(solution)/shard_map/reduce_scatter | solution.py:61
  136.8 3.2 multiply_bitcast_fusion
  140.0 1.6 copy.24
  141.6 10.7 %fusion.28 = f32[256,64,128]{2,1,0:T(8,128)S(1)} fusion(f32[256,64,128]{2,1,0:T(8,128)S(1)} %bitcast.68), kind=kOutput, calls=%fused_computation.43 | convolution fusion | flops 3221798912 | bytes 16777216 | tf_op jit(solution)/shard_map/rab,cb->rac/dot_general | solution.py:37
  152.3 9.7 %convolution_bitcast_fusion = f32[256,64,128]{2,1,0:T(8,128)} fusion(f32[256,64,128]{2,1,0:T(8,128)S(1)} %fusion.28), kind=kOutput, calls=%fused_computation.20 | convolution fusion | flops 1610743808 | bytes 16777216 | tf_op jit(solution)/shard_map/rab,ca->rcb/dot_general | solution.py:40
  162.0 9.3 %copy.23 = f32[256,64,128]{0,2,1:T(8,128)} copy(f32[256,64,128]{2,1,0:T(8,128)} %convolution_bitcast_fusion) | data formatting | bytes 16777216 | tf_op jit(solution)/shard_map/reshape | solution.py:41
  171.3 6.8 %gather_fusion = f32[1024,256]{1,0:T(8,128)S(1)} fusion(f32[256,8192]{0,1:T(8,128)} %bitcast.69, s32[1024]{0:T(1024)S(1)} %get-tuple-element.8), kind=kCustom, calls=%fused_computation | custom fusion | bytes 2101248 | tf_op jit(solution)/shard_map/jit(_take)/gather | solution.py:64
  178.1 1.0 fusion.19
  179.1 23.4 %all-gather.2.cloned.1.call-done = bf16[1024,1024]{0,1:T(8,128)(2,1)} async-done(((bf16[256,1024]{0,1:T(8,128)(2,1)}), bf16[1024,1024]{0,1:T(8,128)(2,1)}) %all-gather.2.cloned.1.call-update) | async-done | bytes 2097168 | tf_op jit(solution)/shard_map/all_gather | solution.py:65
  202.5 3.9 copy.16
  206.4 5.8 %all-to-all-start = ((bf16[1024,8,128]{2,0,1:T(8,128)(2,1)}), bf16[1024,8,128]{2,0,1:T(8,128)(2,1)S(1)}, u32[]{:S(2)}, u32[]{:S(2)}) async-start(bf16[1024,8,128]{2,0,1:T(8,128)(2,1)} %copy.16), calls=%async_computation.1 | async-start | bytes 4194304 | tf_op jit(solution)/shard_map/all_to_all | solution.py:68
  213.1 45.4 %all-to-all-done = bf16[1024,8,128]{2,0,1:T(8,128)(2,1)S(1)} async-done(((bf16[1024,8,128]{2,0,1:T(8,128)(2,1)}), bf16[1024,8,128]{2,0,1:T(8,128)(2,1)S(1)}, u32[]{:S(2)}, u32[]{:S(2)}) %all-to-all-start) | async-done | bytes 2097184 | tf_op jit(solution)/shard_map/all_to_all | solution.py:68
  258.5 0.3 convert_element_type.77
  258.8 4.6 fusion.13
  263.4 6.2 %fusion.9 = f32[64,128,128]{2,0,1:T(8,128)S(1)} fusion(f32[64,128,128]{2,1,0:T(8,128)S(1)} %fusion.13), kind=kOutput, calls=%fused_computation.16 | convolution fusion | flops 805437440 | bytes 8388608 | tf_op jit(solution)/shard_map/abc,da->dbc/dot_general | solution.py:50
  269.7 4.6 copy.18
  274.3 5.0 %gather_fusion.1 = f32[1024,128]{1,0:T(8,128)S(1)} fusion(f32[8192,128]{1,0:T(8,128)} %bitcast.72, s32[1024]{0:T(1024)S(1)} %get-tuple-element.8), kind=kCustom, calls=%fused_computation.1 | custom fusion | bytes 1052672 | tf_op jit(solution)/shard_map/jit(_take)/gather | solution.py:72
  279.4 0.9 multiply_divide_fusion
  280.2 7.5 %all_gather.7 = f32[1024,128]{1,0:T(8,128)S(1)} all-gather(f32[256,128]{1,0:T(8,128)S(1)} %get-tuple-element.3), channel_id=1, replica_groups=mesh['rep'=4,'fsdp'=8] {'rep'}, dimensions={0}, use_global_device_ids=true | all-gather | bytes 655360 | tf_op jit(solution)/shard_map/all_gather | solution.py:82
  287.7 5.3 %scatter_custom_fusion = f32[8192,128]{1,0:T(8,128)} fusion(s32[1024]{0:T(1024)S(1)} %get-tuple-element.9, f32[1024,128]{1,0:T(8,128)S(1)} %all_gather.7, f32[]{:T(128)} %constant.67.clone.1), kind=kCustom, calls=%fused_computation.24 | custom fusion | bytes 4194308 | tf_op jit(solution)/shard_map/scatter | solution.py:83
  293.0 5.6 %convolution_bitcast_fusion.1 = f32[64,128,128]{2,1,0:T(8,128)S(1)} fusion(f32[64,128,128]{2,1,0:T(8,128)} %bitcast.73), kind=kOutput, calls=%fused_computation.22 | convolution fusion | flops 1611186176 | bytes 8388608 | tf_op jit(solution)/shard_map/abc,db->adc/dot_general | solution.py:49
  298.6 6.0 %fusion.7 = f32[64,128,128]{2,0,1:T(8,128)S(1)} fusion(f32[64,128,128]{2,1,0:T(8,128)S(1)} %convolution_bitcast_fusion.1), kind=kOutput, calls=%fused_computation.14 | convolution fusion | flops 805437440 | bytes 8388608 | tf_op jit(solution)/shard_map/abc,da->dbc/dot_general | solution.py:50
  304.5 2.4 copy.20
  307.0 1.4 fusion.6
  308.4 52.1 %all_to_all.29 = bf16[8,1024,128]{2,1,0:T(8,128)(2,1)S(1)} all-to-all(bf16[8,1024,128]{2,1,0:T(8,128)(2,1)S(1)} %fusion.6), channel_id=1, replica_groups=mesh['rep'=4,'fsdp'=8] {'fsdp'}, dimensions={0} | all-to-all | bytes 4194304 | tf_op jit(solution)/shard_map/all_to_all | solution.py:85
  360.5 2.6 copy.21
  363.1 15.6 %scatter_custom_fusion.1 = bf16[1024,8192]{0,1:T(8,128)(2,1)} fusion(s32[1024]{0:T(1024)S(1)} %get-tuple-element.9, bf16[1024,1024]{1,0:T(8,128)(2,1)} %bitcast.77, bf16[]{:T(256)} %constant.64.clone.1), kind=kCustom, calls=%fused_computation.9 | custom fusion | bytes 16777728 | tf_op jit(solution)/shard_map/scatter | solution.py:87
  378.7 22.8 %copy.22 = bf16[1024,64,128]{2,1,0:T(8,128)(2,1)} copy(bf16[1024,64,128]{0,2,1:T(8,128)(2,1)} %bitcast.67) | data formatting | bytes 33554432 | tf_op jit(solution)/shard_map/reshape | solution.py:28
  401.5 16.6 %fusion.35 = f32[1024,64,128]{2,1,0:T(8,128)} fusion(bf16[1024,64,128]{2,1,0:T(8,128)(2,1)} %copy.22), kind=kOutput, calls=%fused_computation.53 | convolution fusion | flops 2148073472 | bytes 50331648 | tf_op jit(solution)/shard_map/rab,cb->rac/dot_general | solution.py:30
  418.1 36.5 %fusion.42 = f32[64,1024,128]{2,0,1:T(8,128)} fusion(f32[1024,64,128]{2,1,0:T(8,128)} %fusion.35), kind=kOutput, calls=%fused_computation.57 | convolution fusion | flops 6442582016 | bytes 67108864 | tf_op jit(solution)/shard_map/rab,ca->rcb/dot_general | solution.py:40
  454.6 26.2 %fusion.2 = bf16[1024,8192]{1,0:T(8,128)(2,1)} fusion(f32[128,8,64,128]{3,2,1,0:T(8,128)} %bitcast.66, bf16[1024,8192]{1,0:T(8,128)(2,1)} %param.8, f32[8192]{0:T(1024)S(1)} %get-tuple-element.7), kind=kLoop, calls=%fused_computation.7 | loop fusion | flops 41943040 | bytes 67141632 | tf_op jit(solution)/shard_map/convert_element_type | solution.py:90
  (16 shorter events, 0.2 us)
Async XLA Ops:
  7.2 129.6 %reduce-scatter.2.cloned.1.call-start = ((), (), s32[]{:S(2)}) async-start(), calls=%async_computation.3 | async-start | bytes 20971520 | tf_op jit(solution)/shard_map/reduce_scatter | solution.py:61
  7.2 0.7 copy-start.3
  7.2 0.8 copy-start.2
  7.9 194.6 %all-gather.2.cloned.1.call-start = ((), (), s32[]{:S(2)}) async-start(), calls=%async_computation.4 | async-start | bytes 2621440 | tf_op jit(solution)/shard_map/all_gather | solution.py:65
  206.4 52.1 %all-to-all-start = ((bf16[1024,8,128]{2,0,1:T(8,128)(2,1)}), bf16[1024,8,128]{2,0,1:T(8,128)(2,1)S(1)}, u32[]{:S(2)}, u32[]{:S(2)}) async-start(bf16[1024,8,128]{2,0,1:T(8,128)(2,1)} %copy.16), calls=%async_computation.1 | async-start | bytes 4194304 | tf_op jit(solution)/shard_map/all_to_all | solution.py:68
  274.3 5.0 %copy-start = (f32[256,128]{1,0:T(8,128)S(1)}, f32[256,128]{1,0:T(8,128)}, u32[]{:S(2)}) copy-start(f32[256,128]{1,0:T(8,128)} %param.10) | copy-start | bytes 393220
  274.3 5.1 %copy-start.1 = (f32[256,128]{1,0:T(8,128)S(1)}, f32[256,128]{1,0:T(8,128)}, u32[]{:S(2)}) copy-start(f32[256,128]{1,0:T(8,128)} %param.9) | copy-start | bytes 393220
Sparse Core Ops, SparseCore 0:
  10.6 126.1 reduce-scatter.1
  179.3 23.2 all-gather.1
where the time goes:
time: 496 us; the launch traced here: 488 us
  waiting for transfers between devices  198 us (40%)
  matrix products  95.9 us (19%)
  local copies, waits for them, and re-layouts  80.2 us (16%)
  blocking collectives  59.6 us (12%)
  other arithmetic  33 us (7%)
  between operations  15.1 us (3%)
  starting transfers between devices  5.89 us (1%)
    reduce_scatter x1, waiting for transfers between devices, local(): lax.psum_scatter(local_grads.astype(jnp.float32).astype(jnp.bfloat16), 'r...  129 us
    all_to_all x1, blocking collectives, local(): lax.all_to_all(back_bf, 'fsdp', split_axis=0, concat_axis=1, tiled=True)  52.1 us
    dot_general x2, matrix products, transform_last(): jnp.einsum('rab,ca->rcb', values, hadamard(high_len), precision=lax.Preci...  46.2 us
    all_to_all x1, waiting for transfers between devices, local(): lax.all_to_all(row_block.astype(jnp.bfloat16), 'fsdp', split_axis=1, conc...  45.4 us
    convert_element_type x1, other arithmetic, local(): (weight.astype(jnp.float32) - LEARN_RATE * update_full).astype(jnp.bfloat16)  26.2 us
    all_gather x1, waiting for transfers between devices, local(): lax.all_gather(row_part.astype(jnp.bfloat16), 'rep', axis=0, tiled=True)  23.4 us
    reshape x1, local copies, waits for them, and re-layouts, transform_last(): values = matrix.reshape(matrix.shape[:-1] + (high_len, low_len))  22.8 us
    dot_general x1, matrix products, transform_last(): jnp.einsum('rab,cb->rac', values, hadamard(low_len).astype(jnp.bfloat16),...  16.6 us
  transfers between devices with their start and end apart: 3, of which 3 were waited for; matrix products, arithmetic and copies ran while one was open for 0% of the time, Pallas kernels for 0%

commit v1 on v0

v1 whole, which is shorter than its diff:
```python
import math

import jax
import jax.numpy as jnp
from jax import lax
from jax.sharding import PartitionSpec as P

BETA_ONE = 0.9
BETA_TWO = 0.95
EPSILON = 1e-08
LEARN_RATE = 0.25


def sketch(kept_rows, signs, start, length, scale):
    columns = start + jnp.arange(length, dtype=jnp.int32)
    both = jnp.bitwise_and(kept_rows[:, None], columns[None, :])
    odd = jnp.bitwise_and(lax.population_count(both) + signs[None, :], 1)
    return jnp.where(odd == 1, -scale, scale).astype(jnp.bfloat16)


def local(replica_grads, weight, moment_one, moment_two, sign_bits, kept_rows, step_count):
    full_len = sign_bits.shape[0]
    kept_len = kept_rows.shape[0]
    scale = 1.0 / math.sqrt(kept_len)
    rows = weight.shape[0]
    start = lax.axis_index("fsdp") * rows
    whole = sketch(kept_rows, sign_bits, 0, full_len, scale)
    mine = sketch(
        kept_rows, lax.dynamic_slice_in_dim(sign_bits, start, rows, 0), start, rows, scale
    )
    grads = replica_grads[0]
    right = lax.dot_general(
        grads, whole, (((1,), (1,)), ((), ())), preferred_element_type=jnp.float32
    ).astype(jnp.bfloat16)
    part = lax.dot_general(
        mine, right, (((1,), (0,)), ((), ())), preferred_element_type=jnp.float32
    ).astype(jnp.bfloat16)
    part = lax.psum_scatter(part, "rep", scatter_dimension=0, tiled=True)
    compressed = lax.psum_scatter(part, "fsdp", scatter_dimension=1, tiled=True).astype(
        jnp.float32
    )
    new_one = BETA_ONE * moment_one + (1.0 - BETA_ONE) * compressed
    new_two = BETA_TWO * moment_two + (1.0 - BETA_TWO) * compressed * compressed
    steps_done = step_count.astype(jnp.float32)
    first_fix = 1.0 - jnp.power(jnp.float32(BETA_ONE), steps_done)
    second_fix = 1.0 - jnp.power(jnp.float32(BETA_TWO), steps_done)
    direction = new_one / first_fix / (jnp.sqrt(new_two / second_fix) + EPSILON)
    panel = lax.all_gather(direction.astype(jnp.bfloat16), "fsdp", axis=1, tiled=True)
    panel = lax.all_gather(panel, "rep", axis=0, tiled=True)
    back = lax.dot_general(
        mine, panel, (((0,), (0,)), ((), ())), preferred_element_type=jnp.float32
    ).astype(jnp.bfloat16)
    update = lax.dot_general(
        back, whole, (((1,), (0,)), ((), ())), preferred_element_type=jnp.float32
    )
    new_weight = (weight.astype(jnp.float32) - LEARN_RATE * update).astype(jnp.bfloat16)
    return (new_weight, new_one, new_two)


def solution(mesh):
    in_specs = (
        P("rep", "fsdp", None),
        P("fsdp", None),
        P("rep", "fsdp"),
        P("rep", "fsdp"),
        P(),
        P(),
        P(),
    )
    out_specs = (P("fsdp", None), P("rep", "fsdp"), P("rep", "fsdp"))
    return jax.shard_map(local, mesh=mesh, in_specs=in_specs, out_specs=out_specs, check_vma=False)
```

time: 496 us -> 221 us (0.45); the launches traced: 488 us -> 219 us
  local copies, waits for them, and re-layouts: 80.2 us -> 3.71 us
  waiting for transfers between devices: 198 us -> 122 us
  matrix products: 95.9 us -> 54.6 us
  blocking collectives: 59.6 us -> 23.1 us
  other arithmetic: 33 us -> 0.79 us
  starting transfers between devices: 5.89 us -> 0.12 us
    reduce_scatter x1, waiting for transfers between devices: 129 us -> 31.6 us  [local(): part = lax.psum_scatter(part, 'rep', scatter_dimension=0, tiled=True)]
    unnamed x2 -> x4, waiting for transfers between devices: 0.68 us -> 60.8 us
    all_to_all x1 -> x0, blocking collectives: 52.1 us -> none  [local(): lax.all_to_all(back_bf, 'fsdp', split_axis=0, concat_axis=1, tiled=True)]
    all_to_all x1 -> x0, waiting for transfers between devices: 45.4 us -> none  [local(): lax.all_to_all(row_block.astype(jnp.bfloat16), 'fsdp', split_axis=1, conc...]
    dot_general x8 -> x4, matrix products: 95.9 us -> 54.6 us  [the longest x1 23.6 us: local(): lax.dot_general(back, whole, (((1,), (0,)), ((), ())), preferred_element_...]
    reshape x2 -> x0, local copies, waits for them, and re-layouts: 32.1 us -> none  [the longest x1 22.8 us: transform_last(): values = matrix.reshape(matrix.shape[:-1] + (high_len, low_len))]
    convert_element_type x4 -> x1, other arithmetic: 28.9 us -> 0.79 us  [local(): direction.astype(jnp.bfloat16)]
    scatter x2 -> x0, local copies, waits for them, and re-layouts: 20.9 us -> none  [the longest x1 15.6 us: local(): jnp.zeros((back_rows.shape[0], full_len), jnp.bfloat16).at[:, kept_rows]]
where the time goes in v1:
time: 221 us; the launch traced here: 219 us
  waiting for transfers between devices  122 us (55%)
  matrix products  54.6 us (25%)
  blocking collectives  23.1 us (10%)
  between operations  14.6 us (7%)
  local copies, waits for them, and re-layouts  3.71 us (2%)
    unnamed x4, waiting for transfers between devices  60.8 us
    reduce_scatter x1, waiting for transfers between devices, local(): part = lax.psum_scatter(part, 'rep', scatter_dimension=0, tiled=True)  31.6 us
    all_gather x1, waiting for transfers between devices, local(): panel = lax.all_gather(panel, 'rep', axis=0, tiled=True)  29.4 us
    dot_general x1, matrix products, local(): lax.dot_general(back, whole, (((1,), (0,)), ((), ())), preferred_element_...  23.6 us
    all_gather x1, blocking collectives, local(): lax.all_gather(direction.astype(jnp.bfloat16), 'fsdp', axis=1, tiled=True)  23.1 us
    dot_general x1, matrix products, local(): lax.dot_general(grads, whole, (((1,), (1,)), ((), ())), preferred_element...  23.1 us
  transfers between devices with their start and end apart: 3, of which 3 were waited for; matrix products, arithmetic and copies ran while one was open for 0% of the time, Pallas kernels for 0%

profile of v1, /device:TPU:31, one launch (start us, length us, event | category | flops | bytes accessed | tf_op | source)
XLA Modules:
  0.0 218.5 jit_solution(13743935407426267511)
XLA Ops:
  7.2 0.0 reduce-scatter.5.cloned.1.call-start
  7.2 0.7 dynamic_slice.3
  7.9 0.0 copy-start.3
  7.9 23.1 %fusion = bf16[1024,1024]{1,0:T(8,128)(2,1)S(1)} fusion(bf16[1,1024,8192]{2,1,0:T(8,128)(2,1)} %param.7, s32[8192]{0:T(1024)} %param.11, s32[1024]{0:T(1024)} %param.12), kind=kOutput, calls=%fused_computation.3 | convolution fusion | flops 17238589440 | bytes 18911232 | tf_op jit(solution)/shard_map/dot_general | solution.py:32
  31.0 0.0 copy-done.3
  31.0 0.0 copy-start
  31.0 0.0 copy-start.1
  31.0 3.7 %fusion.6 = bf16[1024,1024]{1,0:T(8,128)(2,1)} fusion(bf16[1024,1024]{1,0:T(8,128)(2,1)S(1)} %fusion, s32[1024]{0:T(1024)S(1)} %dynamic_slice.3, s32[1024]{0:T(1024)S(1)} %iota_add_fusion, s32[1024]{0:T(1024)S(1)} %copy-done.3), kind=kOutput, calls=%fused_computation.11 | convolution fusion | flops 2155872256 | bytes 4206592 | tf_op jit(solution)/shard_map/dot_general | solution.py:35
  34.7 0.0 reduce-scatter.5.cloned.1.call-update
  34.8 0.0 reduce-scatter.7.cloned.1.call-start
  34.8 31.6 %reduce-scatter.5.cloned.1.call-done = bf16[256,1024]{1,0:T(8,128)(2,1)} async-done(((bf16[1024,1024]{1,0:T(8,128)(2,1)}), bf16[256,1024]{1,0:T(8,128)(2,1)}) %reduce-scatter.5.cloned.1.call-update) | async-done | bytes 524304 | tf_op jit(solution)/shard_map/reduce_scatter | solution.py:38
  66.4 2.0 copy.10
  68.4 0.0 reduce-scatter.7.cloned.1.call-update
  68.4 0.0 all-gather.2.cloned.1.call-start
  69.2 60.7 %reduce-scatter.7.cloned.1.call-done = bf16[128,256]{1,0:T(8,128)(2,1)} async-done(((bf16[1024,256]{1,0:T(8,128)(2,1)}), bf16[128,256]{1,0:T(8,128)(2,1)}) %reduce-scatter.7.cloned.1.call-update) | async-done | bytes 65552
  130.0 0.9 copy.11
  130.9 0.0 copy-done
  130.9 0.0 copy-done.1
  130.9 0.8 divide_convert_fusion
  131.7 23.1 %all_gather.6 = bf16[256,1024]{1,0:T(8,128)(2,1)} all-gather(bf16[256,128]{1,0:T(8,128)(2,1)S(1)} %get-tuple-element.3), channel_id=1, replica_groups=mesh['rep'=4,'fsdp'=8] {'fsdp'}, dimensions={1}, use_global_device_ids=true | all-gather | bytes 589824 | tf_op jit(solution)/shard_map/all_gather | solution.py:48
  154.8 0.0 all-gather.2.cloned.1.call-update
  154.8 0.0 copy-start.2
  154.8 29.4 %all-gather.2.cloned.1.call-done = bf16[1024,1024]{1,0:T(8,128)(2,1)} async-done(((bf16[256,1024]{1,0:T(8,128)(2,1)}), bf16[1024,1024]{1,0:T(8,128)(2,1)}) %all-gather.2.cloned.1.call-update) | async-done | bytes 2097168 | tf_op jit(solution)/shard_map/all_gather | solution.py:49
  184.2 4.2 %fusion.34 = bf16[1024,1024]{1,0:T(8,128)(2,1)S(1)} fusion(bf16[1024,1024]{1,0:T(8,128)(2,1)} %all-gather.2.cloned.1.call-done, s32[1024]{0:T(1024)S(1)} %dynamic_slice.3, s32[1024]{0:T(1024)S(1)} %iota_add_fusion, s32[1024]{0:T(1024)S(1)} %copy-done.3), kind=kOutput, calls=%fused_computation.7.clone.2 | convolution fusion | flops 2155872256 | bytes 4206592 | tf_op jit(solution)/shard_map/dot_general | solution.py:50
  188.4 0.0 copy-done.2
  188.4 23.6 %subtract_convert_fusion = bf16[1024,8192]{1,0:T(8,128)(2,1)} fusion(bf16[1024,8192]{1,0:T(8,128)(2,1)} %param.8, s32[8192]{0:T(1024)S(1)} %copy-done.2, s32[1024]{0:T(1024)S(1)} %copy-done.3, bf16[1024,1024]{1,0:T(8,128)(2,1)S(1)} %fusion.34), kind=kOutput, calls=%fused_computation | convolution fusion | flops 17272143872 | bytes 35688448 | tf_op jit(solution)/shard_map/dot_general | solution.py:53
  (1 shorter events, 0.0 us)
Async XLA Ops:
  7.2 59.2 %reduce-scatter.5.cloned.1.call-start = ((), (), s32[]{:S(2)}) async-start(), calls=%async_computation.2 | async-start | bytes 2621440 | tf_op jit(solution)/shard_map/reduce_scatter | solution.py:38
  7.9 23.1 %copy-start.3 = (s32[1024]{0:T(1024)S(1)}, s32[1024]{0:T(1024)}, u32[]{:S(2)}) copy-start(s32[1024]{0:T(1024)} %param.12) | copy-start | bytes 12292
  31.0 99.9 %copy-start = (f32[256,128]{1,0:T(8,128)S(1)}, f32[256,128]{1,0:T(8,128)}, u32[]{:S(2)}) copy-start(f32[256,128]{1,0:T(8,128)} %param.10) | copy-start | bytes 393220
  31.0 99.9 %copy-start.1 = (f32[256,128]{1,0:T(8,128)S(1)}, f32[256,128]{1,0:T(8,128)}, u32[]{:S(2)}) copy-start(f32[256,128]{1,0:T(8,128)} %param.9) | copy-start | bytes 393220
  34.8 95.2 %reduce-scatter.7.cloned.1.call-start = ((), (), s32[]{:S(2)}) async-start(), calls=%async_computation.4 | async-start | bytes 589824
  68.4 115.8 %all-gather.2.cloned.1.call-start = ((), (), s32[]{:S(2)}) async-start(), calls=%async_computation.3 | async-start | bytes 2621440 | tf_op jit(solution)/shard_map/all_gather | solution.py:49
  154.8 33.6 %copy-start.2 = (s32[8192]{0:T(1024)S(1)}, s32[8192]{0:T(1024)}, u32[]{:S(2)}) copy-start(s32[8192]{0:T(1024)} %param.11) | copy-start | bytes 98308
Sparse Core Ops, SparseCore 0:
  34.9 31.4 reduce-scatter.4
  70.7 59.2 reduce-scatter.6
  154.9 29.2 all-gather.1

commit v2 on v1

--- a/solution.py
+++ b/solution.py
@@ -1,8 +1,11 @@
+import functools
 import math
 
 import jax
 import jax.numpy as jnp
 from jax import lax
+from jax.experimental import pallas as pl
+from jax.experimental.pallas import tpu as pltpu
 from jax.sharding import PartitionSpec as P
 
 BETA_ONE = 0.9
@@ -18,7 +21,134 @@
     return jnp.where(odd == 1, -scale, scale).astype(jnp.bfloat16)
 
 
-def local(replica_grads, weight, moment_one, moment_two, sign_bits, kept_rows, step_count):
+def adam(compressed, moment_one, moment_two, first_fix, second_fix):
+    new_one = BETA_ONE * moment_one + (1.0 - BETA_ONE) * compressed
+    new_two = BETA_TWO * moment_two + (1.0 - BETA_TWO) * compressed * compressed
+    direction = new_one / first_fix / (jnp.sqrt(new_two / second_fix) + EPSILON)
+    return new_one, new_two, direction.astype(jnp.bfloat16)
+
+
+def exchange(
+    wide, tall, part, one, two, fixes, panel, new_one, new_two,
+    got_core, sum_core, got_x, sum_x, got_y, sum_y, got_z, gathered, send, recv,
+):
+    rep, fsdp = lax.axis_index("rep"), lax.axis_index("fsdp")
+    x, core = rep // 2, rep % 2
+    z, y = fsdp // 2, fsdp % 2
+    width = one.shape[1]
+    at_core = (x * 2 + (1 - core), fsdp)
+    at_x = [(lax.rem(x + d, wide) * 2 + core, fsdp) for d in range(1, wide)]
+    at_y = (rep, z * 2 + (1 - y))
+    at_z = [(rep, lax.rem(z + d, tall) * 2 + y) for d in range(1, tall)]
+    partners = [at_core, at_y] + at_x + at_z
+    barrier = pltpu.get_barrier_semaphore()
+    for partner in partners:
+        pl.semaphore_signal(
+            barrier, inc=1, device_id=partner, device_id_type=pl.DeviceIdType.MESH
+        )
+    pl.semaphore_wait(barrier, len(partners))
+
+    used = [0]
+
+    def copy(source, target, partner):
+        index = used[0]
+        used[0] += 1
+        made = pltpu.make_async_remote_copy(
+            src_ref=source,
+            dst_ref=target,
+            send_sem=send.at[index],
+            recv_sem=recv.at[index],
+            device_id=partner,
+            device_id_type=pl.DeviceIdType.MESH,
+        )
+        made.start()
+        return made
+
+    def finish(copies):
+        for made in copies:
+            made.wait()
+
+    def add(left, *others):
+        total = left.astype(jnp.float32)
+        for other in others:
+            total = total + other.astype(jnp.float32)
+        return total
+
+    finish([copy(part.at[:, 1 - core], got_core, at_core)])
+    for i in range(wide):
+        sum_core[i] = add(part[i, core], got_core[i]).astype(jnp.bfloat16)
+    finish(
+        [
+            copy(sum_core.at[lax.rem(x + d, wide)], got_x.at[d - 1], at_x[d - 1])
+            for d in range(1, wide)
+        ]
+    )
+    for i in range(2 * tall):
+        columns = slice(i * width, (i + 1) * width)
+        sum_x[i // 2, i % 2] = add(
+            sum_core[x, :, columns], *[got_x[d, :, columns] for d in range(wide - 1)]
+        ).astype(jnp.bfloat16)
+    finish([copy(sum_x.at[:, 1 - y], got_y, at_y)])
+    for i in range(tall):
+        sum_y[i] = add(sum_x[i, y], got_y[i]).astype(jnp.bfloat16)
+    finish(
+        [
+            copy(sum_y.at[lax.rem(z + d, tall)], got_z.at[d - 1], at_z[d - 1])
+            for d in range(1, tall)
+        ]
+    )
+    compressed = add(sum_y[z], *[got_z[d] for d in range(tall - 1)])
+    new_one[...], new_two[...], gathered[z, y] = adam(
+        compressed, one[...], two[...], fixes[0], fixes[1]
+    )
+    finish(
+        [copy(gathered.at[z, y], gathered.at[z, y], at_z[d - 1]) for d in range(1, tall)]
+    )
+    finish([copy(gathered.at[:, y], gathered.at[:, y], at_y)])
+    for i in range(2 * tall):
+        panel[x, core, :, i * width : (i + 1) * width] = gathered[i // 2, i % 2]
+    finish([copy(panel.at[x, core], panel.at[x, core], at_x[d - 1]) for d in range(1, wide)])
+    finish([copy(panel.at[:, core], panel.at[:, core], at_core)])
+
+
+def exchanged(reps, shards, part, moment_one, moment_two, fixes):
+    wide, tall = reps // 2, shards // 2
+    height, width = moment_one.shape
+    length = part.shape[1]
+    half = jnp.bfloat16
+    panel, new_one, new_two = pl.pallas_call(
+        functools.partial(exchange, wide, tall),
+        out_shape=(
+            jax.ShapeDtypeStruct((wide, 2, height, length), half),
+            jax.ShapeDtypeStruct((height, width), jnp.float32),
+            jax.ShapeDtypeStruct((height, width), jnp.float32),
+        ),
+        in_specs=[pl.BlockSpec(memory_space=pltpu.VMEM)] * 3
+        + [pl.BlockSpec(memory_space=pltpu.SMEM)],
+        out_specs=(pl.BlockSpec(memory_space=pltpu.VMEM),) * 3,
+        scratch_shapes=[
+            pltpu.VMEM((wide, height, length), half),
+            pltpu.VMEM((wide, height, length), half),
+            pltpu.VMEM((max(wide - 1, 1), height, length), half),
+            pltpu.VMEM((tall, 2, height, width), half),
+            pltpu.VMEM((tall, height, width), half),
+            pltpu.VMEM((tall, height, width), half),
+            pltpu.VMEM((max(tall - 1, 1), height, width), half),
+            pltpu.VMEM((tall, 2, height, width), half),
+            pltpu.SemaphoreType.DMA((2 * (wide + tall),)),
+            pltpu.SemaphoreType.DMA((2 * (wide + tall),)),
+        ],
+        compiler_params=pltpu.CompilerParams(
+            collective_id=0, has_side_effects=True, vmem_limit_bytes=24 * 2**20
+        ),
+        cost_estimate=pl.CostEstimate(
+            flops=8 * height * length, bytes_accessed=6 * part.size, transcendentals=0
+        ),
+    )(part.reshape(wide, 2, height, length), moment_one, moment_two, fixes)
+    return panel.reshape(part.shape), new_one, new_two
+
+
+def local(reps, shards, replica_grads, weight, moment_one, moment_two, sign_bits, kept_rows, step_count):
     full_len = sign_bits.shape[0]
     kept_len = kept_rows.shape[0]
     scale = 1.0 / math.sqrt(kept_len)
@@ -35,18 +165,23 @@
     part = lax.dot_general(
         mine, right, (((1,), (0,)), ((), ())), preferred_element_type=jnp.float32
     ).astype(jnp.bfloat16)
-    part = lax.psum_scatter(part, "rep", scatter_dimension=0, tiled=True)
-    compressed = lax.psum_scatter(part, "fsdp", scatter_dimension=1, tiled=True).astype(
-        jnp.float32
-    )
-    new_one = BETA_ONE * moment_one + (1.0 - BETA_ONE) * compressed
-    new_two = BETA_TWO * moment_two + (1.0 - BETA_TWO) * compressed * compressed
     steps_done = step_count.astype(jnp.float32)
     first_fix = 1.0 - jnp.power(jnp.float32(BETA_ONE), steps_done)
     second_fix = 1.0 - jnp.power(jnp.float32(BETA_TWO), steps_done)
-    direction = new_one / first_fix / (jnp.sqrt(new_two / second_fix) + EPSILON)
-    panel = lax.all_gather(direction.astype(jnp.bfloat16), "fsdp", axis=1, tiled=True)
-    panel = lax.all_gather(panel, "rep", axis=0, tiled=True)
+    height, width = moment_one.shape
+    if reps % 2 == 0 and shards % 2 == 0 and height % 16 == 0 and width % 128 == 0:
+        fixes = jnp.stack([first_fix, second_fix])
+        panel, new_one, new_two = exchanged(reps, shards, part, moment_one, moment_two, fixes)
+    else:
+        part = lax.psum_scatter(part, "rep", scatter_dimension=0, tiled=True)
+        compressed = lax.psum_scatter(part, "fsdp", scatter_dimension=1, tiled=True).astype(
+            jnp.float32
+        )
+        new_one, new_two, block = adam(
+            compressed, moment_one, moment_two, first_fix, second_fix
+        )
+        panel = lax.all_gather(block, "fsdp", axis=1, tiled=True)
+        panel = lax.all_gather(panel, "rep", axis=0, tiled=True)
     back = lax.dot_general(
         mine, panel, (((0,), (0,)), ((), ())), preferred_element_type=jnp.float32
     ).astype(jnp.bfloat16)
@@ -68,4 +203,5 @@
         P(),
     )
     out_specs = (P("fsdp", None), P("rep", "fsdp"), P("rep", "fsdp"))
-    return jax.shard_map(local, mesh=mesh, in_specs=in_specs, out_specs=out_specs, check_vma=False)
+    run = functools.partial(local, mesh.shape["rep"], mesh.shape["fsdp"])
+    return jax.shard_map(run, mesh=mesh, in_specs=in_specs, out_specs=out_specs, check_vma=False)

time: 221 us -> 116 us (0.52); the launches traced: 219 us -> 116 us
  waiting for transfers between devices: 122 us -> 0 us
  Pallas kernels: 0 us -> 62.5 us
  blocking collectives: 23.1 us -> 0 us
  between operations: 14.6 us -> 1.52 us
  matrix products: 54.6 us -> 49.8 us
    pallas_call x0 -> x1, Pallas kernels: none -> 62.5 us  [exchanged(): pl.pallas_call(functools.partial(exchange, wide, tall), out_shape=(jax.Sh...]
    unnamed x4 -> x0, waiting for transfers between devices: 60.8 us -> none
    reduce_scatter x1 -> x0, waiting for transfers between devices: 31.6 us -> none  [local(): part = lax.psum_scatter(part, 'rep', scatter_dimension=0, tiled=True)]
    all_gather x1 -> x0, waiting for transfers between devices: 29.4 us -> none  [local(): panel = lax.all_gather(panel, 'rep', axis=0, tiled=True)]
    all_gather x1 -> x0, blocking collectives: 23.1 us -> none  [local(): lax.all_gather(direction.astype(jnp.bfloat16), 'fsdp', axis=1, tiled=True)]
  transfers between devices with their start and end apart: 3 -> 0, of which waited for: 3 -> 0; matrix products, arithmetic and copies ran while one was open for 0% -> 0% of each run, Pallas kernels for 0% -> 0%
where the time goes in v2:
time: 116 us
  Pallas kernels  62.5 us (54%)
  matrix products  49.8 us (43%)
  local copies, waits for them, and re-layouts  2.05 us (2%)
  between operations  1.52 us (1%)
    pallas_call x1, Pallas kernels, exchanged(): pl.pallas_call(functools.partial(exchange, wide, tall), out_shape=(jax.Sh...  62.5 us
    dot_general x1, matrix products, local(): lax.dot_general(grads, whole, (((1,), (1,)), ((), ())), preferred_element...  23.2 us
    dot_general x1, matrix products, local(): lax.dot_general(back, whole, (((1,), (0,)), ((), ())), preferred_element_...  21.6 us
    dot_general x1, matrix products, local(): lax.dot_general(mine, panel, (((0,), (0,)), ((), ())), preferred_element_...  2.58 us
    dot_general x1, matrix products, local(): lax.dot_general(mine, right, (((1,), (0,)), ((), ())), preferred_element_...  2.39 us

profile of v2, /device:TPU:31, one launch (start us, length us, event | category | flops | bytes accessed | tf_op | source)
XLA Modules:
  0.0 116.0 jit_solution(825879422217438895)
XLA Ops:
  1.4 0.1 pad_maximum_fusion.fixes
  1.4 0.7 dynamic_slice.3
  2.1 0.0 copy-start.3
  2.1 23.2 %fusion = bf16[1024,1024]{1,0:T(8,128)(2,1)S(1)} fusion(bf16[1,1024,8192]{2,1,0:T(8,128)(2,1)} %param.7, s32[8192]{0:T(1024)} %param.11, s32[1024]{0:T(1024)} %param.12), kind=kOutput, calls=%fused_computation.3 | convolution fusion | flops 17238589440 | bytes 18911232 | tf_op jit(solution)/shard_map/dot_general | solution.py:162
  25.4 0.0 copy-done.3
  25.4 0.0 copy-start
  25.4 0.0 copy-start.1
  25.4 0.0 slice-start
  25.4 0.0 slice-start.1
  25.4 0.0 slice-start.2
  25.4 2.4 %fusion.6 = bf16[1024,1024]{1,0:T(8,128)(2,1)S(1)} fusion(bf16[1024,1024]{1,0:T(8,128)(2,1)S(1)} %fusion, s32[1024]{0:T(1024)S(1)} %dynamic_slice.3, s32[1024]{0:T(1024)S(1)} %iota_add_fusion, s32[1024]{0:T(1024)S(1)} %copy-done.3), kind=kOutput, calls=%fused_computation.11 | convolution fusion | flops 2155872256 | bytes 4206592 | tf_op jit(solution)/shard_map/dot_general | solution.py:165
  27.8 0.0 copy-done
  27.8 0.0 copy-done.1
  27.9 62.5 %shard_map.94 = (bf16[2,2,256,1024]{3,2,1,0:T(8,128)(2,1)S(1)}, f32[256,128]{1,0:T(8,128)S(1)}, f32[256,128]{1,0:T(8,128)S(1)}) custom-call(bf16[2,2,256,1024]{3,2,1,0:T(8,128)(2,1)S(1)} %bitcast.14, f32[256,128]{1,0:T(8,128)S(1)} %copy-done, f32[256,128]{1,0:T(8,128)S(1)} %copy-done.1, f32[2]{0:T(128)S(1)} %pad_maximum_fusion.fixes), custom_call_target="tpu_custom_call" | custom-call | flops 2097152 | bytes 6291456 | tf_op jit(solution)/shard_map/pallas_call | solution.py:119
  90.4 0.0 copy-start.2
  90.4 0.0 slice-start.3
  90.4 2.6 %fusion.30 = bf16[1024,1024]{1,0:T(8,128)(2,1)S(1)} fusion(bf16[1024,1024]{1,0:T(8,128)(2,1)S(1)} %bitcast.15, s32[1024]{0:T(1024)S(1)} %dynamic_slice.3, s32[1024]{0:T(1024)S(1)} %iota_add_fusion, s32[1024]{0:T(1024)S(1)} %copy-done.3), kind=kOutput, calls=%fused_computation.7.clone.2 | convolution fusion | flops 2155872256 | bytes 4206592 | tf_op jit(solution)/shard_map/dot_general | solution.py:185
  93.0 0.0 slice-done
  93.0 0.0 slice-done.1
  93.0 0.0 slice-done.2
  93.0 0.0 copy-done.2
  93.0 0.0 slice-done.3
  93.1 21.6 %subtract_convert_fusion = bf16[1024,8192]{1,0:T(8,128)(2,1)} fusion(bf16[1024,8192]{1,0:T(8,128)(2,1)S(1)} %bitcast.17, s32[8192]{0:T(1024)S(1)} %copy-done.2, s32[1024]{0:T(1024)S(1)} %copy-done.3, bf16[1024,1024]{1,0:T(8,128)(2,1)S(1)} %fusion.30), kind=kOutput, calls=%fused_computation | convolution fusion | flops 17272143872 | bytes 35688448 | tf_op jit(solution)/shard_map/dot_general | solution.py:188
  114.6 0.7 copy.13
  115.3 0.7 copy.14
  (2 shorter events, 0.0 us)
Async XLA Ops:
  2.1 23.2 %copy-start.3 = (s32[1024]{0:T(1024)S(1)}, s32[1024]{0:T(1024)}, u32[]{:S(2)}) copy-start(s32[1024]{0:T(1024)} %param.12) | copy-start | bytes 12292
  25.4 2.5 %copy-start = (f32[256,128]{1,0:T(8,128)S(1)}, f32[256,128]{1,0:T(8,128)}, u32[]{:S(2)}) copy-start(f32[256,128]{1,0:T(8,128)} %one.1) | copy-start | bytes 393220
  25.4 2.5 %copy-start.1 = (f32[256,128]{1,0:T(8,128)S(1)}, f32[256,128]{1,0:T(8,128)}, u32[]{:S(2)}) copy-start(f32[256,128]{1,0:T(8,128)} %two.1) | copy-start | bytes 393220
  25.4 67.6 %slice-start = ((s8[16777216]{0:T(1024)(128)(4,1)}), s8[4194304]{0:T(1024)(128)(4,1)S(1)}, s32[]{:S(2)}) async-start(s8[16777216]{0:T(1024)(128)(4,1)} %bitcast.16), calls=%async_computation | async-start | bytes 8388608
  25.4 67.6 %slice-start.1 = ((s8[16777216]{0:T(1024)(128)(4,1)}), s8[4194304]{0:T(1024)(128)(4,1)S(1)}, s32[]{:S(2)}) async-start(s8[16777216]{0:T(1024)(128)(4,1)} %bitcast.16), calls=%async_computation.1 | async-start | bytes 8388608
  25.4 67.6 %slice-start.2 = ((s8[16777216]{0:T(1024)(128)(4,1)}), s8[4194304]{0:T(1024)(128)(4,1)S(1)}, s32[]{:S(2)}) async-start(s8[16777216]{0:T(1024)(128)(4,1)} %bitcast.16), calls=%async_computation.2 | async-start | bytes 8388608
  90.4 2.6 %copy-start.2 = (s32[8192]{0:T(1024)S(1)}, s32[8192]{0:T(1024)}, u32[]{:S(2)}) copy-start(s32[8192]{0:T(1024)} %param.11) | copy-start | bytes 98308
  90.4 2.6 %slice-start.3 = ((s8[16777216]{0:T(1024)(128)(4,1)}), s8[4194304]{0:T(1024)(128)(4,1)S(1)}, s32[]{:S(2)}) async-start(s8[16777216]{0:T(1024)(128)(4,1)} %bitcast.16), calls=%async_computation.3 | async-start | bytes 8388608

commit v3 on v2

--- a/solution.py
+++ b/solution.py
@@ -76,21 +76,32 @@
 
     finish([copy(part.at[:, 1 - core], got_core, at_core)])
     for i in range(wide):
-        sum_core[i] = add(part[i, core], got_core[i]).astype(jnp.bfloat16)
-    finish(
+        for j in range(2 * tall):
+            columns = slice(j * width, (j + 1) * width)
+            sum_core[i, j % 2, j // 2] = add(
+                part[i, core, :, columns], got_core[i, :, columns]
+            ).astype(jnp.bfloat16)
+    passed, kept = [
         [
-            copy(sum_core.at[lax.rem(x + d, wide)], got_x.at[d - 1], at_x[d - 1])
+            copy(sum_core.at[lax.rem(x + d, wide), v], got_x.at[d - 1, v], at_x[d - 1])
             for d in range(1, wide)
         ]
-    )
-    for i in range(2 * tall):
-        columns = slice(i * width, (i + 1) * width)
-        sum_x[i // 2, i % 2] = add(
-            sum_core[x, :, columns], *[got_x[d, :, columns] for d in range(wide - 1)]
+        for v in (1 - y, y)
+    ]
+    finish(passed)
+    for i in range(tall):
+        sum_x[1 - y, i] = add(
+            sum_core[x, 1 - y, i], *[got_x[d, 1 - y, i] for d in range(wide - 1)]
         ).astype(jnp.bfloat16)
-    finish([copy(sum_x.at[:, 1 - y], got_y, at_y)])
+    across = copy(sum_x.at[1 - y], got_y, at_y)
+    finish(kept)
     for i in range(tall):
-        sum_y[i] = add(sum_x[i, y], got_y[i]).astype(jnp.bfloat16)
+        sum_x[y, i] = add(
+            sum_core[x, y, i], *[got_x[d, y, i] for d in range(wide - 1)]
+        ).astype(jnp.bfloat16)
+    finish([across])
+    for i in range(tall):
+        sum_y[i] = add(sum_x[y, i], got_y[i]).astype(jnp.bfloat16)
     finish(
         [
             copy(sum_y.at[lax.rem(z + d, tall)], got_z.at[d - 1], at_z[d - 1])
@@ -98,16 +109,20 @@
         ]
     )
     compressed = add(sum_y[z], *[got_z[d] for d in range(tall - 1)])
-    new_one[...], new_two[...], gathered[z, y] = adam(
+    new_one[...], new_two[...], gathered[x, y, z] = adam(
         compressed, one[...], two[...], fixes[0], fixes[1]
     )
-    finish(
-        [copy(gathered.at[z, y], gathered.at[z, y], at_z[d - 1]) for d in range(1, tall)]
-    )
-    finish([copy(gathered.at[:, y], gathered.at[:, y], at_y)])
-    for i in range(2 * tall):
-        panel[x, core, :, i * width : (i + 1) * width] = gathered[i // 2, i % 2]
-    finish([copy(panel.at[x, core], panel.at[x, core], at_x[d - 1]) for d in range(1, wide)])
+    mine = gathered.at[x, y, z]
+    finish([copy(mine, mine, at_z[d - 1]) for d in range(1, tall)])
+    mine, other = gathered.at[x, y], gathered.at[x, 1 - y]
+    across = copy(mine, mine, at_y)
+    along = [copy(mine, mine, at_x[d - 1]) for d in range(1, wide)]
+    finish([across])
+    along += [copy(other, other, at_x[d - 1]) for d in range(1, wide)]
+    finish(along)
+    for i in range(wide):
+        for j in range(2 * tall):
+            panel[i, core, :, j * width : (j + 1) * width] = gathered[i, j % 2, j // 2]
     finish([copy(panel.at[:, core], panel.at[:, core], at_core)])
 
 
@@ -128,15 +143,15 @@
         out_specs=(pl.BlockSpec(memory_space=pltpu.VMEM),) * 3,
         scratch_shapes=[
             pltpu.VMEM((wide, height, length), half),
-            pltpu.VMEM((wide, height, length), half),
-            pltpu.VMEM((max(wide - 1, 1), height, length), half),
-            pltpu.VMEM((tall, 2, height, width), half),
+            pltpu.VMEM((wide, 2, tall, height, width), half),
+            pltpu.VMEM((max(wide - 1, 1), 2, tall, height, width), half),
+            pltpu.VMEM((2, tall, height, width), half),
             pltpu.VMEM((tall, height, width), half),
             pltpu.VMEM((tall, height, width), half),
             pltpu.VMEM((max(tall - 1, 1), height, width), half),
-            pltpu.VMEM((tall, 2, height, width), half),
-            pltpu.SemaphoreType.DMA((2 * (wide + tall),)),
-            pltpu.SemaphoreType.DMA((2 * (wide + tall),)),
+            pltpu.VMEM((wide, 2, tall, height, width), half),
+            pltpu.SemaphoreType.DMA((2 * (2 * wide + tall),)),
+            pltpu.SemaphoreType.DMA((2 * (2 * wide + tall),)),
         ],
         compiler_params=pltpu.CompilerParams(
             collective_id=0, has_side_effects=True, vmem_limit_bytes=24 * 2**20

time: 116 us -> 104 us (0.90)
  Pallas kernels: 62.5 us -> 50.9 us
    pallas_call x1, Pallas kernels: 62.5 us -> 50.9 us  [exchanged(): pl.pallas_call(functools.partial(exchange, wide, tall), out_shape=(jax.Sh...]
where the time goes in v3:
time: 104 us
  Pallas kernels  50.9 us (49%)
  matrix products  49.8 us (48%)
  local copies, waits for them, and re-layouts  2.05 us (2%)
  between operations  1.52 us (1%)
    pallas_call x1, Pallas kernels, exchanged(): pl.pallas_call(functools.partial(exchange, wide, tall), out_shape=(jax.Sh...  50.9 us
    dot_general x1, matrix products, local(): lax.dot_general(grads, whole, (((1,), (1,)), ((), ())), preferred_element...  23.2 us
    dot_general x1, matrix products, local(): lax.dot_general(back, whole, (((1,), (0,)), ((), ())), preferred_element_...  21.6 us
    dot_general x1, matrix products, local(): lax.dot_general(mine, panel, (((0,), (0,)), ((), ())), preferred_element_...  2.58 us
    dot_general x1, matrix products, local(): lax.dot_general(mine, right, (((1,), (0,)), ((), ())), preferred_element_...  2.39 us

profile of v3, /device:TPU:31, one launch (start us, length us, event | category | flops | bytes accessed | tf_op | source)
XLA Modules:
  0.0 104.3 jit_solution(9818637248153045343)
XLA Ops:
  1.4 0.1 pad_maximum_fusion.fixes
  1.4 0.7 dynamic_slice.3
  2.1 0.0 copy-start.3
  2.1 23.2 %fusion = bf16[1024,1024]{1,0:T(8,128)(2,1)S(1)} fusion(bf16[1,1024,8192]{2,1,0:T(8,128)(2,1)} %param.7, s32[8192]{0:T(1024)} %param.11, s32[1024]{0:T(1024)} %param.12), kind=kOutput, calls=%fused_computation.3 | convolution fusion | flops 17238589440 | bytes 18911232 | tf_op jit(solution)/shard_map/dot_general | solution.py:177
  25.4 0.0 copy-done.3
  25.4 0.0 copy-start
  25.4 0.0 copy-start.1
  25.4 0.0 slice-start
  25.4 0.0 slice-start.1
  25.4 0.0 slice-start.2
  25.4 2.4 %fusion.6 = bf16[1024,1024]{1,0:T(8,128)(2,1)S(1)} fusion(bf16[1024,1024]{1,0:T(8,128)(2,1)S(1)} %fusion, s32[1024]{0:T(1024)S(1)} %dynamic_slice.3, s32[1024]{0:T(1024)S(1)} %iota_add_fusion, s32[1024]{0:T(1024)S(1)} %copy-done.3), kind=kOutput, calls=%fused_computation.11 | convolution fusion | flops 2155872256 | bytes 4206592 | tf_op jit(solution)/shard_map/dot_general | solution.py:180
  27.8 0.0 copy-done
  27.8 0.0 copy-done.1
  27.9 50.9 %shard_map.94 = (bf16[2,2,256,1024]{3,2,1,0:T(8,128)(2,1)S(1)}, f32[256,128]{1,0:T(8,128)S(1)}, f32[256,128]{1,0:T(8,128)S(1)}) custom-call(bf16[2,2,256,1024]{3,2,1,0:T(8,128)(2,1)S(1)} %bitcast.14, f32[256,128]{1,0:T(8,128)S(1)} %copy-done, f32[256,128]{1,0:T(8,128)S(1)} %copy-done.1, f32[2]{0:T(128)S(1)} %pad_maximum_fusion.fixes), custom_call_target="tpu_custom_call" | custom-call | flops 2097152 | bytes 6291456 | tf_op jit(solution)/shard_map/pallas_call | solution.py:134
  78.7 0.0 copy-start.2
  78.7 0.0 slice-start.3
  78.8 2.6 %fusion.30 = bf16[1024,1024]{1,0:T(8,128)(2,1)S(1)} fusion(bf16[1024,1024]{1,0:T(8,128)(2,1)S(1)} %bitcast.15, s32[1024]{0:T(1024)S(1)} %dynamic_slice.3, s32[1024]{0:T(1024)S(1)} %iota_add_fusion, s32[1024]{0:T(1024)S(1)} %copy-done.3), kind=kOutput, calls=%fused_computation.7.clone.2 | convolution fusion | flops 2155872256 | bytes 4206592 | tf_op jit(solution)/shard_map/dot_general | solution.py:200
  81.3 0.0 slice-done
  81.3 0.0 slice-done.1
  81.4 0.0 slice-done.2
  81.4 0.0 copy-done.2
  81.4 0.0 slice-done.3
  81.4 21.6 %subtract_convert_fusion = bf16[1024,8192]{1,0:T(8,128)(2,1)} fusion(bf16[1024,8192]{1,0:T(8,128)(2,1)S(1)} %bitcast.17, s32[8192]{0:T(1024)S(1)} %copy-done.2, s32[1024]{0:T(1024)S(1)} %copy-done.3, bf16[1024,1024]{1,0:T(8,128)(2,1)S(1)} %fusion.30), kind=kOutput, calls=%fused_computation | convolution fusion | flops 17272143872 | bytes 35688448 | tf_op jit(solution)/shard_map/dot_general | solution.py:203
  103.0 0.7 copy.13
  103.6 0.7 copy.14
  (2 shorter events, 0.0 us)
Async XLA Ops:
  2.1 23.2 %copy-start.3 = (s32[1024]{0:T(1024)S(1)}, s32[1024]{0:T(1024)}, u32[]{:S(2)}) copy-start(s32[1024]{0:T(1024)} %param.12) | copy-start | bytes 12292
  25.4 2.5 %copy-start = (f32[256,128]{1,0:T(8,128)S(1)}, f32[256,128]{1,0:T(8,128)}, u32[]{:S(2)}) copy-start(f32[256,128]{1,0:T(8,128)} %one.1) | copy-start | bytes 393220
  25.4 2.5 %copy-start.1 = (f32[256,128]{1,0:T(8,128)S(1)}, f32[256,128]{1,0:T(8,128)}, u32[]{:S(2)}) copy-start(f32[256,128]{1,0:T(8,128)} %two.1) | copy-start | bytes 393220
  25.4 55.9 %slice-start = ((s8[16777216]{0:T(1024)(128)(4,1)}), s8[4194304]{0:T(1024)(128)(4,1)S(1)}, s32[]{:S(2)}) async-start(s8[16777216]{0:T(1024)(128)(4,1)} %bitcast.16), calls=%async_computation | async-start | bytes 8388608
  25.4 55.9 %slice-start.1 = ((s8[16777216]{0:T(1024)(128)(4,1)}), s8[4194304]{0:T(1024)(128)(4,1)S(1)}, s32[]{:S(2)}) async-start(s8[16777216]{0:T(1024)(128)(4,1)} %bitcast.16), calls=%async_computation.1 | async-start | bytes 8388608
  25.4 55.9 %slice-start.2 = ((s8[16777216]{0:T(1024)(128)(4,1)}), s8[4194304]{0:T(1024)(128)(4,1)S(1)}, s32[]{:S(2)}) async-start(s8[16777216]{0:T(1024)(128)(4,1)} %bitcast.16), calls=%async_computation.2 | async-start | bytes 8388608
  78.7 2.6 %copy-start.2 = (s32[8192]{0:T(1024)S(1)}, s32[8192]{0:T(1024)}, u32[]{:S(2)}) copy-start(s32[8192]{0:T(1024)} %param.11) | copy-start | bytes 98308
  78.7 2.6 %slice-start.3 = ((s8[16777216]{0:T(1024)(128)(4,1)}), s8[4194304]{0:T(1024)(128)(4,1)S(1)}, s32[]{:S(2)}) async-start(s8[16777216]{0:T(1024)(128)(4,1)} %bitcast.16), calls=%async_computation.3 | async-start | bytes 8388608
